TPU v7x, 32 devices: a whole 2x2x4 slice. The times are simulated.
32 devices in a mesh: blk: 4 (over x, core), uly: 8 (over z, y).
Axes of the slice: x: 2, y: 2, z: 4, core: 2. Of those that a mesh axis runs over, the one named last changes fastest.
Arguments:
- video: bfloat16 [6144, 3072], P(('blk', 'uly')), may hold values from -6 to 6
- w_qkv: bfloat16 [3072, 3072], P(None, 'uly'), may hold values from -0.109375 to 0.109375
- w_out: bfloat16 [1024, 3072], P('uly'), may hold values from -0.5 to 0.5
- q_gain: float32 [128], replicated, may hold values from 0.6 to 12
- k_gain: float32 [128], replicated, may hold values from 0.6 to 12
- tile_blocks: int32 [96, 27], P('blk'), may hold values from 0 to 95, as said below
- tile_counts: int32 [96], P('blk'), may hold values from 1 to 27
Outputs:
- mixed: bfloat16 [6144, 3072], P(('blk', 'uly'))
Inputs may be any that keep to these rules, and one draw needn't show every extreme that they name: `tile_blocks`: tile t's list holds distinct tiles whose frame, row and column tile coordinates each differ from t's by at most one, t itself among them, in the order of increasing offset (frame, then row, then column offset from -1 to 1); entries at positions tile_counts[t] and later equal t. Some tile's list is full in every draw.
All inputs are finite; a program needn't handle non-finite values.
Results may differ from a plain program's by a relative error of at most 0.009.
The roundings to bfloat16 on the way count: a program that leaves them out, or rounds other values in their place, can miss the bound.
Values may be sent and summed in bfloat16 or wider, within the bound.
A program may use at most 128 MiB of HBM per device.

v0:
```python
import math

import jax
import jax.numpy as jnp
from jax import lax
from jax.sharding import PartitionSpec as P

MAXB = 27
BLOCK = 64


def with_halo(cells, sides, width):
    for axis, dim in sides:
        count = lax.axis_size(axis)
        ends = count - 1
        head = lax.slice_in_dim(cells, 0, width, axis=dim)
        tail = lax.slice_in_dim(cells, cells.shape[dim] - width, cells.shape[dim], axis=dim)
        cells = jnp.concatenate(
            [
                lax.ppermute(tail, axis, [(i, (i + 1) % count) for i in range(ends)]),
                cells,
                lax.ppermute(head, axis, [((i + 1) % count, i) for i in range(ends)]),
            ],
            axis=dim,
        )
    return cells


def norm_rows(values_in, gain):
    return (
        values_in
        * lax.rsqrt(jnp.mean(values_in * values_in, axis=-1, keepdims=True) + 1e-06)
        * gain
    )


def attend_tiles(query_tiles, gathered, live_keys, head_size):
    key_part = gathered[..., :head_size]
    value_part = gathered[..., head_size:]
    scores = jnp.einsum("tqd,tkd->tqk", query_tiles, key_part, preferred_element_type=jnp.float32)
    scores = jnp.where(live_keys[:, None, :], scores, -jnp.inf)
    largest = jnp.max(scores, axis=-1, keepdims=True)
    weights = jnp.exp(scores - largest)
    running = jnp.sum(weights, axis=-1, keepdims=True)
    rounded = weights.astype(jnp.bfloat16)
    summed = jnp.einsum("tqk,tkd->tqd", rounded, value_part, preferred_element_type=jnp.float32)
    return (summed / running).astype(jnp.bfloat16)


def local(video, w_qkv, w_out, q_gain, k_gain, tile_blocks, tile_counts):
    head_size = w_out.shape[0]
    projected = jnp.dot(
        lax.all_gather(video, "uly", axis=0, tiled=True), w_qkv, preferred_element_type=jnp.float32
    )
    slab_rows = projected.shape[0]
    tiles = slab_rows // BLOCK
    queries = (norm_rows(projected[:, :head_size], q_gain) * head_size ** (-0.5)).astype(
        jnp.bfloat16
    )
    keys_now = norm_rows(projected[:, head_size : 2 * head_size], k_gain).astype(jnp.bfloat16)
    values_now = projected[:, 2 * head_size :].astype(jnp.bfloat16)
    key_value = jnp.concatenate([keys_now, values_now], axis=1)
    extended = with_halo(key_value, (("blk", 0),), slab_rows)
    key_blocks = extended.reshape(3 * tiles, BLOCK, 2 * head_size)
    local_ids = tile_blocks - (lax.axis_index("blk") - 1) * tiles
    slot_index = jnp.arange(MAXB, dtype=jnp.int32)
    live_keys = jnp.repeat(slot_index[None, :] < tile_counts[:, None], BLOCK, axis=1)
    group_size = math.gcd(tiles, 8)
    group_count = tiles // group_size

    def one_group(inputs):
        query_tiles, block_ids, live_now = inputs
        gathered = key_blocks[block_ids].reshape(group_size, MAXB * BLOCK, 2 * head_size)
        return attend_tiles(query_tiles, gathered, live_now, head_size)

    attended = lax.map(
        one_group,
        (
            queries.reshape(group_count, group_size, BLOCK, head_size),
            local_ids.reshape(group_count, group_size, MAXB),
            live_keys.reshape(group_count, group_size, MAXB * BLOCK),
        ),
    )
    attended = attended.reshape(slab_rows, head_size)
    summed = lax.psum_scatter(
        jnp.dot(attended, w_out, preferred_element_type=jnp.float32),
        "uly",
        scatter_dimension=0,
        tiled=True,
    )
    return summed.astype(jnp.bfloat16)


def solution(mesh):
    return jax.shard_map(
        local,
        mesh=mesh,
        in_specs=(
            P(("blk", "uly"), None),
            P(None, "uly"),
            P("uly", None),
            P(),
            P(),
            P("blk", None),
            P("blk"),
        ),
        out_specs=P(("blk", "uly"), None),
        check_vma=False,
    )
```

profile of v0, /device:TPU:1, one launch (start us, length us, event | category | flops | bytes accessed | tf_op | source)
XLA Modules:
  0.0 563.7 jit_solution(7893840119883776479)
XLA Ops:
  7.3 142.0 %all-gather.2.cloned.1.call-done = bf16[1536,3072]{1,0:T(8,128)(2,1)} async-done(((bf16[192,3072]{1,0:T(8,128)(2,1)}), bf16[1536,3072]{1,0:T(8,128)(2,1)}) %all-gather.2.cloned.1.call-update) | async-done | bytes 9437200 | tf_op jit(solution)/shard_map/all_gather | solution.py:53
  149.3 7.5 %fusion.34 = f32[1536,384]{1,0:T(8,128)S(1)} fusion(bf16[1536,3072]{1,0:T(8,128)(2,1)} %all-gather.2.cloned.1.call-done, bf16[3072,384]{1,0:T(8,128)(2,1)S(1)} %copy-done), kind=kOutput, calls=%fused_computation.34 | convolution fusion | flops 3623878656 | bytes 14155776 | tf_op jit(solution)/shard_map/dot_general | solution.py:52
  157.4 1.1 multiply_convert_fusion
  158.6 1.0 pad_maximum_fusion.1
  159.5 3.0 collective-permute-start.1
  162.5 3.0 collective-permute-start
  167.1 1.7 reshape_reshape.3
  169.4 4.2 collective-permute-done.1
  173.6 1.2 collective-permute-done
  174.8 3.0 pad_maximum_fusion
  177.8 54.8 %while.10 = (s32[]{:T(128)}, bf16[3,8,64,128]{3,2,1,0:T(8,128)(2,1)}, pred[3,8,1728]{2,1,0:T(8,128)(4,1)}, bf16[3,8,64,128]{3,2,1,0:T(8,128)(2,1)S(1)}, s32[3,8,...) while((s32[]{:T(128)}, bf16[3,8,64,128]{3,2,1,0:T(8,128)(2,1)}, pred[3,8,1728]{2,1,0:T(8,128)(4,1)}, ...), condition=%wide.region_5.6_spmd, body=%wide.region_2.5_spmd.sunk | while | flops 460194432 | bytes 60649152 | solution.py:76
  179.9 10.1 %gather_fusion = bf16[216,64,256]{2,1,0:T(8,128)(2,1)} fusion(bf16[72,64,256]{2,1,0:T(8,128)(2,1)} %get-tuple-element.118, s32[1024]{0:T(1024)} %pad_clamp_fusion.2), kind=kCustom, calls=%fused_computation.clone.1 | custom fusion | bytes 14156640 | tf_op jit(solution)/shard_map/while/body/eval_jaxpr/gather | solution.py:73
  190.1 3.5 select_reduce_fusion.2
  193.6 0.9 fusion.46
  194.5 1.6 fusion.47
  198.2 10.1 %gather_fusion = bf16[216,64,256]{2,1,0:T(8,128)(2,1)} fusion(bf16[72,64,256]{2,1,0:T(8,128)(2,1)} %get-tuple-element.118, s32[1024]{0:T(1024)} %pad_clamp_fusion.2), kind=kCustom, calls=%fused_computation.clone.1 | custom fusion | bytes 14156640 | tf_op jit(solution)/shard_map/while/body/eval_jaxpr/gather | solution.py:73
  208.3 3.5 select_reduce_fusion.2
  212.7 1.6 fusion.47
  216.5 10.1 %gather_fusion = bf16[216,64,256]{2,1,0:T(8,128)(2,1)} fusion(bf16[72,64,256]{2,1,0:T(8,128)(2,1)} %get-tuple-element.118, s32[1024]{0:T(1024)} %pad_clamp_fusion.2), kind=kCustom, calls=%fused_computation.clone.1 | custom fusion | bytes 14156640 | tf_op jit(solution)/shard_map/while/body/eval_jaxpr/gather | solution.py:73
  226.6 3.5 select_reduce_fusion.2
  231.0 1.6 fusion.47
  232.6 8.8 %fusion.35 = f32[1536,3072]{1,0:T(8,128)} fusion(bf16[1536,128]{1,0:T(8,128)(2,1)} %bitcast.39, bf16[128,3072]{1,0:T(8,128)(2,1)S(1)} %copy-done.2), kind=kOutput, calls=%fused_computation.35 | convolution fusion | flops 1207959552 | bytes 20054016 | tf_op jit(solution)/shard_map/dot_general | solution.py:86
  241.5 312.5 %reduce-scatter.2.cloned.1.call-done = f32[192,3072]{1,0:T(8,128)} async-done(((f32[1536,3072]{1,0:T(8,128)}), f32[192,3072]{1,0:T(8,128)}) %reduce-scatter.2.cloned.1.call-update) | async-done | bytes 2359312 | tf_op jit(solution)/shard_map/reduce_scatter | solution.py:85
  554.0 2.8 convert_element_type.18
  (39 shorter events, 11.5 us)
Async XLA Ops:
  6.5 142.8 %copy-start = (bf16[3072,384]{1,0:T(8,128)(2,1)S(1)}, bf16[3072,384]{1,0:T(8,128)(2,1)}, u32[]{:S(2)}) copy-start(bf16[3072,384]{1,0:T(8,128)(2,1)} %param.10) | copy-start | bytes 7077892
  6.5 142.8 %all-gather.2.cloned.1.call-start = ((), (), s32[]{:S(2)}) async-start(), calls=%async_computation.1 | async-start | bytes 10616832 | tf_op jit(solution)/shard_map/all_gather | solution.py:53
  7.3 150.2 %copy-start.4 = (f32[128]{0:T(128)S(1)}, f32[128]{0:T(128)}, u32[]{:S(2)}) copy-start(f32[128]{0:T(128)} %param.13) | copy-start | bytes 1540
  7.3 546.7 %reduce-scatter.2.cloned.1.call-start = ((), (), s32[]{:S(2)}) async-start(), calls=%async_computation.2 | async-start | bytes 21233664 | tf_op jit(solution)/shard_map/reduce_scatter | solution.py:85
  156.9 11.9 %copy-start.3 = (s32[24,27]{1,0:T(8,128)S(1)}, s32[24,27]{1,0:T(8,128)}, u32[]{:S(2)}) copy-start(s32[24,27]{1,0:T(8,128)} %param.14) | copy-start | bytes 7780
  159.5 14.0 %collective-permute-start.1 = (bf16[1536,256]{1,0:T(8,128)(2,1)}, bf16[1536,256]{1,0:T(8,128)(2,1)}, u32[]{:S(2)}, u32[]{:S(2)}) collective-permute-start(bf16[1536,256]{1,0:T(8,128)(2,1)} %pad_maximum_fusion.1), channel_id=1, source_target_pairs={{8,0},{16,8},{24,16},{9,1},{17,9},{25,17},{10,2},{18,10},{26,18},{... | collective-permute-start | bytes 2359304 | tf_op jit(solution)/shard_map/ppermute | solution.py:22
  162.5 12.2 %collective-permute-start = (bf16[1536,256]{1,0:T(8,128)(2,1)}, bf16[1536,256]{1,0:T(8,128)(2,1)}, u32[]{:S(2)}, u32[]{:S(2)}) collective-permute-start(bf16[1536,256]{1,0:T(8,128)(2,1)} %pad_maximum_fusion.1), channel_id=1, source_target_pairs={{0,8},{8,16},{16,24},{1,9},{9,17},{17,25},{2,10},{10,18},{18,26},{... | collective-permute-start | bytes 2359304 | tf_op jit(solution)/shard_map/ppermute | solution.py:20
  177.8 54.8 %copy-start.2 = (bf16[128,3072]{1,0:T(8,128)(2,1)S(1)}, bf16[128,3072]{1,0:T(8,128)(2,1)}, u32[]{:S(2)}) copy-start(bf16[128,3072]{1,0:T(8,128)(2,1)} %param.11) | copy-start | bytes 2359300
  190.1 4.4 copy-start.1
  208.3 4.4 copy-start.1
  226.6 4.4 copy-start.1
Sparse Core Ops, SparseCore 0:
  9.5 139.7 all-gather.1
  241.6 312.3 reduce-scatter.1
where the time goes:
time: 565 us; the launch traced here: 564 us
  waiting for transfers between devices  461 us (82%)
  local copies, waits for them, and re-layouts  35.3 us (6%)
  matrix products  31.9 us (6%)
  other arithmetic  16.3 us (3%)
  between operations  13.5 us (2%)
  starting transfers between devices  6.01 us (1%)
    reduce_scatter x1, waiting for transfers between devices, local(): lax.psum_scatter(jnp.dot(attended, w_out, preferred_element_type=jnp.floa...  313 us
    all_gather x1, waiting for transfers between devices, local(): lax.all_gather(video, 'uly', axis=0, tiled=True)  142 us
    gather x3, local copies, waits for them, and re-layouts, one_group(): key_blocks[block_ids].reshape(group_size, MAXB * BLOCK, 2 * head_size)  30.3 us
  transfers between devices with their start and end apart: 4, of which 4 were waited for; matrix products, arithmetic and copies ran while one was open for 1% of the time, Pallas kernels for 0%

commit v1 on v0

v1 whole, which is shorter than its diff:
```python
import functools

import jax
import jax.numpy as jnp
from jax import lax
from jax.experimental import pallas as pl
from jax.experimental.pallas import tpu as pltpu
from jax.sharding import PartitionSpec as P

MAXB = 27
BLOCK = 64
CHUNK = 4
MESH = pl.DeviceIdType.MESH
ANY = pl.BlockSpec(memory_space=pl.ANY)


def remote(src, dst, send, recv, blk, uly):
    return pltpu.make_async_remote_copy(
        src_ref=src,
        dst_ref=dst,
        send_sem=send,
        recv_sem=recv,
        device_id=(blk, uly),
        device_id_type=MESH,
    )


def when(cond, fn):
    pl.when(cond)(fn)


def gather_kernel(
    groups,
    video,
    wq,
    wo,
    vid2,
    wq_all,
    wo_all,
    local_sem,
    vs,
    vr,
    zs,
    zr,
    xs,
    xr,
    cs,
    cr,
    ds,
    dr,
    ozs,
    ozr,
    oys,
    oyr,
    ocs,
    ocr,
    ods,
    odr,
):
    blk, uly = lax.axis_index("blk"), lax.axis_index("uly")
    a, y = uly // 2, uly % 2
    c, core = blk % 4, blk % 2
    x_c = c + 2 - 4 * (c // 2)
    xp = blk - c + x_c
    cp = blk + 1 - 2 * core
    yp = uly + 1 - 2 * y
    last = groups - 1
    rows = video.shape[0]
    part = wq.shape[0] // 4
    half = wo.shape[0] // 2

    barrier = pltpu.get_barrier_semaphore()

    def greet(b, u):
        pl.semaphore_signal(barrier, inc=1, device_id=(b, u), device_id_type=MESH)

    greet(xp, uly)
    greet(cp, uly)
    greet(blk, yp)
    when(a > 0, lambda: greet(blk, uly - 2))
    when(a < last, lambda: greet(blk, uly + 2))
    pl.semaphore_wait(barrier, 3 + (a > 0).astype(jnp.int32) + (a < last).astype(jnp.int32))

    def q_at(s, piece):
        return wq_all.at[s, pl.ds(pl.multiple_of(piece * part, 16), part)]

    def o_at(s, side):
        return wo_all.at[s, pl.ds(pl.multiple_of(side * half, 16), half)]

    q_own = wq.at[pl.ds(pl.multiple_of(c * part, 16), part)]
    o_own = wo.at[pl.ds(pl.multiple_of(core * half, 16), half)]
    v_dst = vid2.at[pl.ds(pl.multiple_of(y * rows, 16), rows)]
    v_peer = vid2.at[pl.ds(pl.multiple_of((1 - y) * rows, 16), rows)]

    onward = (uly + 2, uly - 2)
    can_go = (a < last, a > 0)

    def has(d, t):
        return (a >= t) if d == 0 else (a + t <= last)

    def came(d, t):
        return (a - t) if d == 0 else (a + t)

    def goes(d, t):
        return jnp.logical_and(has(d, t), can_go[d])

    for d in range(2):
        when(
            can_go[d],
            lambda d=d: remote(
                q_own, q_at(a, c), zs.at[d, 0], zr.at[d, 0], blk, onward[d]
            ).start(),
        )
    v_copy = remote(video, v_dst, vs, vr, blk, yp)
    v_copy.start()
    mine = [
        pltpu.make_async_copy(wq, wq_all.at[a], local_sem.at[0]),
        pltpu.make_async_copy(video, v_dst, local_sem.at[1]),
        pltpu.make_async_copy(wo, wo_all.at[uly], local_sem.at[2]),
    ]
    for copy in mine:
        copy.start()

    def q_on(d, t):
        return remote(
            q_at(came(d, t), c), q_at(came(d, t), c), zs.at[d, t], zr.at[d, t], blk, onward[d]
        )

    def q_x(d, t):
        r = q_at(came(d, t), c)
        return remote(r, r, xs.at[d, t - 1], xr.at[d, t - 1], xp, uly)

    def q_c(d, t):
        r = q_at(came(d, t), c)
        return remote(r, r, cs.at[d, t - 1], cr.at[d, t - 1], cp, uly)

    def q_d(d, t):
        r = q_at(came(d, t), x_c)
        return remote(r, r, ds.at[d, t - 1], dr.at[d, t - 1], cp, uly)

    def q_in(d, t):
        r = q_at(came(d, t), c)
        return remote(r, r, zs.at[d, t - 1], zr.at[d, t - 1], blk, yp)

    def q_xin(d, t):
        r = q_at(came(d, t), x_c)
        return remote(r, r, xs.at[d, t - 1], xr.at[d, t - 1], xp, uly)

    def q_cin(d, t, piece, s, r):
        ref = q_at(came(d, t), piece)
        return remote(ref, ref, s.at[d, t - 1], r.at[d, t - 1], cp, uly)

    def arrive(d, t):
        q_in(d, t).wait_recv()
        if t < last:
            when(can_go[d], lambda: q_on(d, t).start())
        q_x(d, t).start()
        q_c(d, t).start()

    def cross(d, t):
        q_xin(d, t).wait_recv()
        q_d(d, t).start()

    for t in range(1, last + 1):
        for d in range(2):
            when(has(d, t), lambda d=d, t=t: arrive(d, t))
        if t > 1:
            for d in range(2):
                when(has(d, t - 1), lambda d=d, t=t: cross(d, t - 1))

    def o_slot(d, t, side=None):
        return came(d, t) * 2 + (y if side is None else side)

    def o_on(d, t):
        src = o_own if t == 0 else o_at(o_slot(d, t), core)
        return remote(
            src, o_at(o_slot(d, t), core), ozs.at[d, t], ozr.at[d, t], blk, onward[d]
        )

    def o_in(d, t):
        r = o_at(o_slot(d, t), core)
        return remote(r, r, ozs.at[d, t - 1], ozr.at[d, t - 1], blk, yp)

    def o_y(d, t):
        src = o_own if t == 0 else o_at(o_slot(d, t), core)
        return remote(src, o_at(o_slot(d, t), core), oys.at[d, t], oyr.at[d, t], blk, yp)

    def o_yin(d, t):
        r = o_at(o_slot(d, t, 1 - y), core)
        return remote(r, r, oys.at[d, t], oyr.at[d, t], blk, yp)

    def o_c(d, t):
        r = o_at(o_slot(d, t), core)
        return remote(r, r, ocs.at[d, t - 1], ocr.at[d, t - 1], cp, uly)

    def o_d(d, t):
        r = o_at(o_slot(d, t, 1 - y), core)
        return remote(r, r, ods.at[d, t], odr.at[d, t], cp, uly)

    def o_cin(d, t):
        r = o_at(o_slot(d, t), 1 - core)
        return remote(r, r, ocs.at[d, t - 1], ocr.at[d, t - 1], cp, uly)

    def o_din(d, t):
        r = o_at(o_slot(d, t, 1 - y), 1 - core)
        return remote(r, r, ods.at[d, t], odr.at[d, t], cp, uly)

    def o_arrive(d, t):
        o_in(d, t).wait_recv()
        if t < last:
            when(can_go[d], lambda: o_on(d, t).start())
        o_y(d, t).start()
        o_c(d, t).start()

    def o_cross(d, t):
        o_yin(d, t).wait_recv()
        o_d(d, t).start()

    for d in range(2):
        when(can_go[d], lambda d=d: o_on(d, 0).start())
    o_y(0, 0).start()
    if last > 0:
        for d in range(2):
            when(has(d, last), lambda d=d: cross(d, last))
    for t in range(1, last + 1):
        for d in range(2):
            when(has(d, t), lambda d=d, t=t: o_arrive(d, t))
        if t == 1:
            o_cross(0, 0)
        else:
            for d in range(2):
                when(has(d, t - 1), lambda d=d, t=t: o_cross(d, t - 1))
    for d in range(2):
        when(has(d, last), lambda d=d: o_cross(d, last))

    for copy in mine:
        copy.wait()
    v_copy.wait_send()
    remote(video, v_peer, vs, vr, blk, yp).wait_recv()
    o_y(0, 0).wait_send()
    o_d(0, 0).wait_send()
    o_din(0, 0).wait_recv()
    for d in range(2):
        when(
            can_go[d],
            lambda d=d: remote(
                q_own, q_at(a, c), zs.at[d, 0], zr.at[d, 0], blk, onward[d]
            ).wait_send(),
        )
        when(can_go[d], lambda d=d: o_on(d, 0).wait_send())

        def finish(d, t):
            if t < last:
                when(can_go[d], lambda: q_on(d, t).wait_send())
                when(can_go[d], lambda: o_on(d, t).wait_send())
            q_x(d, t).wait_send()
            q_c(d, t).wait_send()
            q_d(d, t).wait_send()
            q_cin(d, t, c + 1 - 2 * core, cs, cr).wait_recv()
            q_cin(d, t, x_c + 1 - 2 * core, ds, dr).wait_recv()
            o_y(d, t).wait_send()
            o_c(d, t).wait_send()
            o_d(d, t).wait_send()
            o_cin(d, t).wait_recv()
            o_din(d, t).wait_recv()

        for t in range(1, last + 1):
            when(has(d, t), lambda d=d, t=t: finish(d, t))


def gather_weights(video, wq, wo, groups):
    rows = video.shape[0]
    pair = pltpu.SemaphoreType.DMA((2, groups))
    return pl.pallas_call(
        functools.partial(gather_kernel, groups),
        out_shape=(
            jax.ShapeDtypeStruct((2 * rows, video.shape[1]), video.dtype),
            jax.ShapeDtypeStruct((groups,) + wq.shape, wq.dtype),
            jax.ShapeDtypeStruct((2 * groups,) + wo.shape, wo.dtype),
        ),
        in_specs=[ANY] * 3,
        out_specs=(ANY,) * 3,
        scratch_shapes=[
            pltpu.SemaphoreType.DMA((3,)),
            pltpu.SemaphoreType.DMA,
            pltpu.SemaphoreType.DMA,
        ]
        + [pair] * 16,
        compiler_params=pltpu.CompilerParams(collective_id=0, has_side_effects=True),
    )(video, wq, wo)


def exchange_kernel(groups, slabs, q, kv, q_all, kv_all, local_sem, qs, qr, ks, kr, ps, pr, ns, nr):
    blk, uly = lax.axis_index("blk"), lax.axis_index("uly")
    a, y = uly // 2, uly % 2
    has_prev, has_next = blk > 0, blk < slabs - 1

    barrier = pltpu.get_barrier_semaphore()

    def greet(b, u):
        pl.semaphore_signal(barrier, inc=1, device_id=(b, u), device_id_type=MESH)

    for k in range(1, groups):
        greet(blk, ((a + k) % groups) * 2 + y)
    when(has_prev, lambda: greet(blk - 1, uly))
    when(has_next, lambda: greet(blk + 1, uly))
    pl.semaphore_wait(
        barrier, groups - 1 + has_prev.astype(jnp.int32) + has_next.astype(jnp.int32)
    )

    def there(k):
        return (a + k) % groups

    def source(k):
        return (a - k + groups) % groups

    def kv_out(k):
        return remote(
            kv.at[there(k)], kv_all.at[1, a], ks.at[k], kr.at[k], blk, there(k) * 2 + y
        )

    def q_out(k):
        return remote(q.at[there(k)], q_all.at[a], qs.at[k], qr.at[k], blk, there(k) * 2 + y)

    def kv_in(k):
        r = kv_all.at[1, source(k)]
        return remote(r, r, ks.at[k], kr.at[k], blk, there(k) * 2 + y)

    def q_in(k):
        r = q_all.at[source(k)]
        return remote(r, r, qs.at[k], qr.at[k], blk, there(k) * 2 + y)

    def to_prev(k):
        src = kv.at[a] if k == 0 else kv_all.at[1, source(k)]
        return remote(src, kv_all.at[2, source(k)], ps.at[k], pr.at[k], blk - 1, uly)

    def to_next(k):
        src = kv.at[a] if k == 0 else kv_all.at[1, source(k)]
        return remote(src, kv_all.at[0, source(k)], ns.at[k], nr.at[k], blk + 1, uly)

    def from_prev(k):
        r = kv_all.at[0, source(k)]
        return remote(r, r, ns.at[k], nr.at[k], blk - 1, uly)

    def from_next(k):
        r = kv_all.at[2, source(k)]
        return remote(r, r, ps.at[k], pr.at[k], blk + 1, uly)

    for k in range(1, groups):
        kv_out(k).start()
    when(has_prev, lambda: to_prev(0).start())
    when(has_next, lambda: to_next(0).start())
    mine = [
        pltpu.make_async_copy(q.at[a], q_all.at[a], local_sem.at[0]),
        pltpu.make_async_copy(kv.at[a], kv_all.at[1, a], local_sem.at[1]),
    ]
    for copy in mine:
        copy.start()
    for k in range(1, groups):
        q_out(k).start()
    for k in range(1, groups):
        kv_in(k).wait_recv()
        when(has_prev, lambda k=k: to_prev(k).start())
        when(has_next, lambda k=k: to_next(k).start())
    for copy in mine:
        copy.wait()
    for k in range(1, groups):
        kv_out(k).wait_send()
        q_out(k).wait_send()
        q_in(k).wait_recv()
    for k in range(groups):

        def prev_done(k=k):
            to_prev(k).wait_send()
            from_prev(k).wait_recv()

        def next_done(k=k):
            to_next(k).wait_send()
            from_next(k).wait_recv()

        when(has_prev, prev_done)
        when(has_next, next_done)


def exchange_heads(q, kv, groups, slabs):
    sems = pltpu.SemaphoreType.DMA((groups,))
    return pl.pallas_call(
        functools.partial(exchange_kernel, groups, slabs),
        out_shape=(
            jax.ShapeDtypeStruct(q.shape, q.dtype),
            jax.ShapeDtypeStruct((3,) + kv.shape, kv.dtype),
        ),
        in_specs=[ANY] * 2,
        out_specs=(ANY,) * 2,
        scratch_shapes=[pltpu.SemaphoreType.DMA((2,))] + [sems] * 8,
        compiler_params=pltpu.CompilerParams(collective_id=1, has_side_effects=True),
    )(q, kv)


def attend_kernel(head_size, ids, counts, q_ref, kv_ref, out_ref, keys):
    t = pl.program_id(0)
    count = counts[t]
    chunks = (count + CHUNK - 1) // CHUNK
    slots = ids.shape[1]

    def run(n):
        width = n * CHUNK * BLOCK
        for s in range(n * CHUNK):
            tile = ids[t, s]
            keys[s * BLOCK : (s + 1) * BLOCK, :] = kv_ref[
                pl.ds(pl.multiple_of(tile * BLOCK, BLOCK), BLOCK), :
            ]
        scores = lax.dot_general(
            q_ref[...],
            keys[:width, :head_size],
            (((1,), (1,)), ((), ())),
            preferred_element_type=jnp.float32,
        )
        column = lax.broadcasted_iota(jnp.int32, scores.shape, 1)
        scores = jnp.where(column < count * BLOCK, scores, -jnp.inf)
        largest = jnp.max(scores, axis=-1, keepdims=True)
        weights = jnp.exp(scores - largest)
        total = jnp.sum(weights, axis=-1, keepdims=True)
        summed = jnp.dot(
            weights.astype(jnp.bfloat16),
            keys[:width, head_size:],
            preferred_element_type=jnp.float32,
        )
        out_ref[...] = (summed / total).astype(jnp.bfloat16)

    for n in range(1, slots // CHUNK + 1):
        when(chunks == n, lambda n=n: run(n))


def attend(q, kv, ids, counts):
    rows, head_size = q.shape
    return pl.pallas_call(
        functools.partial(attend_kernel, head_size),
        out_shape=jax.ShapeDtypeStruct(q.shape, jnp.bfloat16),
        grid_spec=pltpu.PrefetchScalarGridSpec(
            num_scalar_prefetch=2,
            grid=(rows // BLOCK,),
            in_specs=[
                pl.BlockSpec((BLOCK, head_size), lambda t, i, n: (t, 0)),
                pl.BlockSpec(kv.shape, lambda t, i, n: (0, 0)),
            ],
            out_specs=pl.BlockSpec((BLOCK, head_size), lambda t, i, n: (t, 0)),
            scratch_shapes=[pltpu.VMEM((ids.shape[1] * BLOCK, 2 * head_size), jnp.bfloat16)],
        ),
        compiler_params=pltpu.CompilerParams(vmem_limit_bytes=32 << 20),
    )(ids, counts, q, kv)


def norm_rows(values_in, gain):
    return (
        values_in
        * lax.rsqrt(jnp.mean(values_in * values_in, axis=-1, keepdims=True) + 1e-06)
        * gain
    )


def local(video, w_qkv, w_out, q_gain, k_gain, tile_blocks, tile_counts):
    head_size = w_out.shape[0]
    ranks, slabs = lax.axis_size("uly"), lax.axis_size("blk")
    groups = ranks // 2
    slab_rows = video.shape[0] * ranks
    tiles = slab_rows // BLOCK
    rows2, w_all, wo_all = gather_weights(video, w_qkv, w_out, groups)
    projected = jnp.einsum("td,adn->atn", rows2, w_all, preferred_element_type=jnp.float32)
    queries = (norm_rows(projected[..., :head_size], q_gain) * head_size ** (-0.5)).astype(
        jnp.bfloat16
    )
    keys_now = norm_rows(projected[..., head_size : 2 * head_size], k_gain).astype(jnp.bfloat16)
    values_now = projected[..., 2 * head_size :].astype(jnp.bfloat16)
    key_value = jnp.concatenate([keys_now, values_now], axis=-1)
    q_all, kv_all = exchange_heads(queries, key_value, groups, slabs)
    local_ids = tile_blocks - (lax.axis_index("blk") - 1) * tiles
    slots = -(-MAXB // CHUNK) * CHUNK
    local_ids = jnp.concatenate([local_ids] + [local_ids[:, -1:]] * (slots - MAXB), axis=1)
    attended = attend(
        q_all.reshape(slab_rows, head_size),
        kv_all.reshape(3 * slab_rows, 2 * head_size),
        local_ids,
        tile_counts,
    )
    by_token = lax.all_to_all(
        attended.reshape(ranks, video.shape[0], head_size), "uly", 0, 0, tiled=True
    )
    by_token = by_token.transpose(1, 0, 2).reshape(video.shape[0], ranks * head_size)
    mixed = jnp.dot(
        by_token,
        wo_all.reshape(ranks * head_size, w_out.shape[1]),
        preferred_element_type=jnp.float32,
    )
    return mixed.astype(jnp.bfloat16)


def solution(mesh):
    return jax.shard_map(
        local,
        mesh=mesh,
        in_specs=(
            P(("blk", "uly"), None),
            P(None, "uly"),
            P("uly", None),
            P(),
            P(),
            P("blk", None),
            P("blk"),
        ),
        out_specs=P(("blk", "uly"), None),
        check_vma=False,
    )
```

time: 565 us -> 214 us (0.38)
  waiting for transfers between devices: 461 us -> 0 us
  Pallas kernels: 0 us -> 178 us
  local copies, waits for them, and re-layouts: 35.3 us -> 2.92 us
  matrix products: 31.9 us -> 12.4 us
  blocking collectives: 0 us -> 17.4 us
  other arithmetic: 16.3 us -> 2.77 us
  between operations: 13.5 us -> 0.12 us
  starting transfers between devices: 6.01 us -> 0 us
    reduce_scatter x1 -> x0, waiting for transfers between devices: 313 us -> none  [local(): lax.psum_scatter(jnp.dot(attended, w_out, preferred_element_type=jnp.floa...]
    pallas_call x0 -> x3, Pallas kernels: none -> 178 us  [the longest x1 136 us: gather_weights(): pl.pallas_call(functools.partial(gather_kernel, groups), out_shape=(jax.S...]
    all_gather x1 -> x0, waiting for transfers between devices: 142 us -> none  [local(): lax.all_gather(video, 'uly', axis=0, tiled=True)]
    gather x3 -> x0, local copies, waits for them, and re-layouts: 30.3 us -> none  [one_group(): key_blocks[block_ids].reshape(group_size, MAXB * BLOCK, 2 * head_size)]
    dot_general x8 -> x2, matrix products: 31.9 us -> 12.4 us  [the longest x1 7.13 us: local(): jnp.einsum('td,adn->atn', rows2, w_all, preferred_element_type=jnp.float32)]
    all_to_all x0 -> x1, blocking collectives: none -> 17.4 us  [local(): lax.all_to_all(attended.reshape(ranks, video.shape[0], head_size), 'uly',...]
    ppermute x2 -> x0, starting transfers between devices: 5.97 us -> none  [the longest x1 3 us: with_halo(): lax.ppermute(tail, axis, [(i, (i + 1) % count) for i in range(ends)])]
  transfers between devices with their start and end apart: 4 -> 0, of which waited for: 4 -> 0; matrix products, arithmetic and copies ran while one was open for 1% -> 0% of each run, Pallas kernels for 0% -> 0%
where the time goes in v1:
time: 214 us
  Pallas kernels  178 us (83%)
  blocking collectives  17.4 us (8%)
  matrix products  12.4 us (6%)
  local copies, waits for them, and re-layouts  2.92 us (1%)
  other arithmetic  2.77 us (1%)
    pallas_call x1, Pallas kernels, gather_weights(): pl.pallas_call(functools.partial(gather_kernel, groups), out_shape=(jax.S...  136 us
    pallas_call x1, Pallas kernels, exchange_heads(): pl.pallas_call(functools.partial(exchange_kernel, groups, slabs), out_sha...  30 us
    all_to_all x1, blocking collectives, local(): lax.all_to_all(attended.reshape(ranks, video.shape[0], head_size), 'uly',...  17.4 us
    pallas_call x1, Pallas kernels, attend(): pl.pallas_call(functools.partial(attend_kernel, head_size), out_shape=jax...  12.7 us
    dot_general x1, matrix products, local(): jnp.einsum('td,adn->atn', rows2, w_all, preferred_element_type=jnp.float32)  7.13 us
    dot_general x1, matrix products, local(): jnp.dot(by_token, wo_all.reshape(ranks * head_size, w_out.shape[1]), pref...  5.28 us

profile of v1, /device:TPU:1, one launch (start us, length us, event | category | flops | bytes accessed | tf_op | source)
XLA Modules:
  0.0 213.9 jit_solution(9604059514138348764)
XLA Ops:
  0.0 135.5 %shard_map.73 = (bf16[384,3072]{1,0:T(8,128)(2,1)}, bf16[4,3072,384]{2,1,0:T(8,128)(2,1)}, bf16[8,128,3072]{2,1,0:T(8,128)(2,1)}) custom-call(bf16[192,3072]{1,0:T(8,128)(2,1)} %video.1, bf16[3072,384]{1,0:T(8,128)(2,1)} %wq.1, bf16[128,3072]{1,0:T(8,128)(2,1)} %wo.1), custom_call_target="tpu_custom_call" | custom-call | tf_op jit(solution)/shard_map/pallas_call | solution.py:274
  135.5 7.1 %fusion.3 = f32[4,384,384]{2,1,0:T(8,128)S(1)} fusion(bf16[4,3072,384]{2,1,0:T(8,128)(2,1)} %get-tuple-element.10, bf16[384,3072]{1,0:T(8,128)(2,1)} %get-tuple-element.11), kind=kOutput, calls=%fused_computation.4 | convolution fusion | flops 3623878656 | bytes 14155776 | tf_op jit(solution)/shard_map/td,adn->atn/dot_general | solution.py:469
  142.6 0.0 copy-start.3
  142.7 0.0 copy-start.4
  142.7 0.0 copy-start.5
  142.7 0.5 multiply_reduce_fusion
  143.2 0.1 slice.26
  143.2 0.1 copy-done.3
  143.4 0.1 slice.17
  143.4 0.1 pad_add_fusion.ids
  143.5 0.0 copy-done.4
  143.5 0.0 copy-done.5
  143.6 0.0 copy-start.2
  143.6 1.2 multiply_convert_fusion
  144.8 1.0 pad_maximum_fusion.kv
  145.8 30.0 %shard_map.74 = (bf16[4,384,128]{2,1,0:T(8,128)(2,1)}, bf16[3,4,384,256]{3,2,1,0:T(8,128)(2,1)}) custom-call(bf16[4,384,128]{2,1,0:T(8,128)(2,1)} %get-tuple-element.18.q, bf16[4,384,256]{2,1,0:T(8,128)(2,1)} %pad_maximum_fusion.kv), custom_call_target="tpu_custom_call" | custom-call | tf_op jit(solution)/shard_map/pallas_call | solution.py:387
  175.8 0.0 copy-done.2
  175.8 0.0 copy-start
  175.8 1.7 copy-done
  177.5 0.0 copy-start.1
  177.5 1.0 copy-done.1
  178.5 12.7 %shard_map.75 = bf16[1536,128]{1,0:T(8,128)(2,1)S(1)} custom-call(s32[24,28]{1,0:T(8,128)S(1)} %pad_add_fusion.ids, s32[24]{0:T(128)S(1)} %copy-done.2, bf16[1536,128]{1,0:T(8,128)(2,1)S(1)} %bitcast.21, bf16[4608,256]{1,0:T(8,128)(2,1)S(1)} %bitcast.19), custom_call_target="tpu_custom_call" | custom-call | tf_op jit(solution)/shard_map/pallas_call | solution.py:437
  191.2 17.4 %all_to_all.5 = bf16[8,192,128]{2,1,0:T(8,128)(2,1)S(1)} all-to-all(bf16[8,192,128]{2,1,0:T(8,128)(2,1)S(1)} %bitcast.20), channel_id=1, replica_groups=mesh['blk'=4,'uly'=8] {'uly'}, dimensions={0} | all-to-all | bytes 786432 | tf_op jit(solution)/shard_map/all_to_all | solution.py:486
  208.6 5.3 %fusion = bf16[192,3072]{1,0:T(8,128)(2,1)} fusion(bf16[8,128,3072]{2,1,0:T(8,128)(2,1)} %get-tuple-element.14, bf16[8,192,128]{2,1,0:T(8,128)(2,1)S(1)} %all_to_all.5), kind=kOutput, calls=%fused_computation.1 | convolution fusion | flops 1208549376 | bytes 7864320 | tf_op jit(solution)/shard_map/dot_general | solution.py:490
  (2 shorter events, 0.0 us)
Async XLA Ops:
  142.6 0.7 copy-start.3
  142.7 0.9 copy-start.4
  142.7 0.9 copy-start.5
  143.6 32.3 %copy-start.2 = (s32[24]{0:T(128)S(1)}, s32[24]{0:T(128)}, u32[]{:S(2)}) copy-start(s32[24]{0:T(128)} %counts.1) | copy-start | bytes 292
  175.8 1.7 copy-start
  177.5 1.0 copy-start.1

commit v2 on v1

--- a/solution.py
+++ b/solution.py
@@ -10,6 +10,9 @@
 MAXB = 27
 BLOCK = 64
 CHUNK = 4
+Q_PARTS = 4
+O_PARTS = 2
+V_PARTS = 2
 MESH = pl.DeviceIdType.MESH
 ANY = pl.BlockSpec(memory_space=pl.ANY)
 
@@ -81,16 +84,30 @@
     when(a < last, lambda: greet(blk, uly + 2))
     pl.semaphore_wait(barrier, 3 + (a > 0).astype(jnp.int32) + (a < last).astype(jnp.int32))
 
-    def q_at(s, piece):
-        return wq_all.at[s, pl.ds(pl.multiple_of(piece * part, 16), part)]
-
-    def o_at(s, side):
-        return wo_all.at[s, pl.ds(pl.multiple_of(side * half, 16), half)]
-
-    q_own = wq.at[pl.ds(pl.multiple_of(c * part, 16), part)]
-    o_own = wo.at[pl.ds(pl.multiple_of(core * half, 16), half)]
-    v_dst = vid2.at[pl.ds(pl.multiple_of(y * rows, 16), rows)]
-    v_peer = vid2.at[pl.ds(pl.multiple_of((1 - y) * rows, 16), rows)]
+    q_sub, o_sub = part // Q_PARTS, half // O_PARTS
+
+    def q_at(s, piece, p):
+        return wq_all.at[s, pl.ds(pl.multiple_of(piece * part + p * q_sub, 16), q_sub)]
+
+    def o_at(s, side, p):
+        return wo_all.at[s, pl.ds(pl.multiple_of(side * half + p * o_sub, 16), o_sub)]
+
+    def q_own(p):
+        return wq.at[pl.ds(pl.multiple_of(c * part + p * q_sub, 16), q_sub)]
+
+    def o_own(p):
+        return wo.at[pl.ds(pl.multiple_of(core * half + p * o_sub, 16), o_sub)]
+
+    v_sub = rows // V_PARTS
+
+    def v_out(p):
+        src = video.at[pl.ds(p * v_sub, v_sub)]
+        dst = vid2.at[pl.ds(pl.multiple_of(y * rows + p * v_sub, 16), v_sub)]
+        return remote(src, dst, vs.at[p], vr.at[p], blk, yp)
+
+    def v_in(p):
+        r = vid2.at[pl.ds(pl.multiple_of((1 - y) * rows + p * v_sub, 16), v_sub)]
+        return remote(r, r, vs.at[p], vr.at[p], blk, yp)
 
     onward = (uly + 2, uly - 2)
     can_go = (a < last, a > 0)
@@ -101,176 +118,175 @@
     def came(d, t):
         return (a - t) if d == 0 else (a + t)
 
-    def goes(d, t):
-        return jnp.logical_and(has(d, t), can_go[d])
-
-    for d in range(2):
-        when(
-            can_go[d],
-            lambda d=d: remote(
-                q_own, q_at(a, c), zs.at[d, 0], zr.at[d, 0], blk, onward[d]
-            ).start(),
-        )
-    v_copy = remote(video, v_dst, vs, vr, blk, yp)
-    v_copy.start()
+    def q_on(d, t, p):
+        dst = q_at(came(d, t), c, p)
+        k = t * Q_PARTS + p
+        return remote(q_own(p) if t == 0 else dst, dst, zs.at[d, k], zr.at[d, k], blk, onward[d])
+
+    def q_copy(d, t, p, piece, send, recv, to_blk, to_uly):
+        r = q_at(came(d, t), piece, p)
+        k = (t - 1) * Q_PARTS + p
+        return remote(r, r, send.at[d, k], recv.at[d, k], to_blk, to_uly)
+
+    def q_in(d, t, p):
+        return q_copy(d, t, p, c, zs, zr, blk, yp)
+
+    def q_x(d, t, p):
+        return q_copy(d, t, p, c, xs, xr, xp, uly)
+
+    def q_xin(d, t, p):
+        return q_copy(d, t, p, x_c, xs, xr, xp, uly)
+
+    def q_c(d, t, p):
+        return q_copy(d, t, p, c, cs, cr, cp, uly)
+
+    def q_cin(d, t, p):
+        return q_copy(d, t, p, c + 1 - 2 * core, cs, cr, cp, uly)
+
+    def q_d(d, t, p):
+        return q_copy(d, t, p, x_c, ds, dr, cp, uly)
+
+    def q_din(d, t, p):
+        return q_copy(d, t, p, x_c + 1 - 2 * core, ds, dr, cp, uly)
+
+    def o_copy(d, t, p, slot, side, send, recv, to_blk, to_uly, own=False):
+        r = o_at(slot, side, p)
+        k = t * O_PARTS + p
+        return remote(o_own(p) if own else r, r, send.at[d, k], recv.at[d, k], to_blk, to_uly)
+
+    def o_on(d, t, p):
+        return o_copy(d, t, p, came(d, t) * 2 + y, core, ozs, ozr, blk, onward[d], t == 0)
+
+    def o_in(d, t, p):
+        return o_copy(d, t - 1, p, came(d, t) * 2 + y, core, ozs, ozr, blk, yp)
+
+    def o_y(d, t, p):
+        return o_copy(d, t, p, came(d, t) * 2 + y, core, oys, oyr, blk, yp, t == 0)
+
+    def o_yin(d, t, p):
+        return o_copy(d, t, p, came(d, t) * 2 + 1 - y, core, oys, oyr, blk, yp)
+
+    def o_c(d, t, p):
+        return o_copy(d, t, p, came(d, t) * 2 + y, core, ocs, ocr, cp, uly)
+
+    def o_cin(d, t, p):
+        return o_copy(d, t, p, came(d, t) * 2 + y, 1 - core, ocs, ocr, cp, uly)
+
+    def o_d(d, t, p):
+        return o_copy(d, t, p, came(d, t) * 2 + 1 - y, core, ods, odr, cp, uly)
+
+    def o_din(d, t, p):
+        return o_copy(d, t, p, came(d, t) * 2 + 1 - y, 1 - core, ods, odr, cp, uly)
+
+    def q_arrive(d, t, p):
+        q_in(d, t, p).wait_recv()
+        if t < last:
+            when(can_go[d], lambda: q_on(d, t, p).start())
+        q_x(d, t, p).start()
+        q_c(d, t, p).start()
+
+    def q_cross(d, t, p):
+        q_xin(d, t, p).wait_recv()
+        q_d(d, t, p).start()
+
+    def o_arrive(d, t, p):
+        o_in(d, t, p).wait_recv()
+        if t < last:
+            when(can_go[d], lambda: o_on(d, t, p).start())
+        o_y(d, t, p).start()
+        o_c(d, t, p).start()
+
+    def o_cross(d, t, p):
+        o_yin(d, t, p).wait_recv()
+        o_d(d, t, p).start()
+
+    def each(cond, parts, fn):
+        def body():
+            for p in range(parts):
+                fn(p)
+
+        when(cond, body)
+
+    for p in range(Q_PARTS):
+        for d in range(2):
+            when(can_go[d], lambda d=d, p=p: q_on(d, 0, p).start())
+    for p in range(V_PARTS):
+        v_out(p).start()
+    for p in range(O_PARTS):
+        o_y(0, 0, p).start()
     mine = [
         pltpu.make_async_copy(wq, wq_all.at[a], local_sem.at[0]),
-        pltpu.make_async_copy(video, v_dst, local_sem.at[1]),
+        pltpu.make_async_copy(
+            video, vid2.at[pl.ds(pl.multiple_of(y * rows, 16), rows)], local_sem.at[1]
+        ),
         pltpu.make_async_copy(wo, wo_all.at[uly], local_sem.at[2]),
     ]
     for copy in mine:
         copy.start()
 
-    def q_on(d, t):
-        return remote(
-            q_at(came(d, t), c), q_at(came(d, t), c), zs.at[d, t], zr.at[d, t], blk, onward[d]
-        )
-
-    def q_x(d, t):
-        r = q_at(came(d, t), c)
-        return remote(r, r, xs.at[d, t - 1], xr.at[d, t - 1], xp, uly)
-
-    def q_c(d, t):
-        r = q_at(came(d, t), c)
-        return remote(r, r, cs.at[d, t - 1], cr.at[d, t - 1], cp, uly)
-
-    def q_d(d, t):
-        r = q_at(came(d, t), x_c)
-        return remote(r, r, ds.at[d, t - 1], dr.at[d, t - 1], cp, uly)
-
-    def q_in(d, t):
-        r = q_at(came(d, t), c)
-        return remote(r, r, zs.at[d, t - 1], zr.at[d, t - 1], blk, yp)
-
-    def q_xin(d, t):
-        r = q_at(came(d, t), x_c)
-        return remote(r, r, xs.at[d, t - 1], xr.at[d, t - 1], xp, uly)
-
-    def q_cin(d, t, piece, s, r):
-        ref = q_at(came(d, t), piece)
-        return remote(ref, ref, s.at[d, t - 1], r.at[d, t - 1], cp, uly)
-
-    def arrive(d, t):
-        q_in(d, t).wait_recv()
-        if t < last:
-            when(can_go[d], lambda: q_on(d, t).start())
-        q_x(d, t).start()
-        q_c(d, t).start()
-
-    def cross(d, t):
-        q_xin(d, t).wait_recv()
-        q_d(d, t).start()
-
     for t in range(1, last + 1):
-        for d in range(2):
-            when(has(d, t), lambda d=d, t=t: arrive(d, t))
-        if t > 1:
+        for p in range(Q_PARTS):
             for d in range(2):
-                when(has(d, t - 1), lambda d=d, t=t: cross(d, t - 1))
-
-    def o_slot(d, t, side=None):
-        return came(d, t) * 2 + (y if side is None else side)
-
-    def o_on(d, t):
-        src = o_own if t == 0 else o_at(o_slot(d, t), core)
-        return remote(
-            src, o_at(o_slot(d, t), core), ozs.at[d, t], ozr.at[d, t], blk, onward[d]
-        )
-
-    def o_in(d, t):
-        r = o_at(o_slot(d, t), core)
-        return remote(r, r, ozs.at[d, t - 1], ozr.at[d, t - 1], blk, yp)
-
-    def o_y(d, t):
-        src = o_own if t == 0 else o_at(o_slot(d, t), core)
-        return remote(src, o_at(o_slot(d, t), core), oys.at[d, t], oyr.at[d, t], blk, yp)
-
-    def o_yin(d, t):
-        r = o_at(o_slot(d, t, 1 - y), core)
-        return remote(r, r, oys.at[d, t], oyr.at[d, t], blk, yp)
-
-    def o_c(d, t):
-        r = o_at(o_slot(d, t), core)
-        return remote(r, r, ocs.at[d, t - 1], ocr.at[d, t - 1], cp, uly)
-
-    def o_d(d, t):
-        r = o_at(o_slot(d, t, 1 - y), core)
-        return remote(r, r, ods.at[d, t], odr.at[d, t], cp, uly)
-
-    def o_cin(d, t):
-        r = o_at(o_slot(d, t), 1 - core)
-        return remote(r, r, ocs.at[d, t - 1], ocr.at[d, t - 1], cp, uly)
-
-    def o_din(d, t):
-        r = o_at(o_slot(d, t, 1 - y), 1 - core)
-        return remote(r, r, ods.at[d, t], odr.at[d, t], cp, uly)
-
-    def o_arrive(d, t):
-        o_in(d, t).wait_recv()
-        if t < last:
-            when(can_go[d], lambda: o_on(d, t).start())
-        o_y(d, t).start()
-        o_c(d, t).start()
-
-    def o_cross(d, t):
-        o_yin(d, t).wait_recv()
-        o_d(d, t).start()
-
+                when(has(d, t), lambda d=d, p=p, t=t: q_arrive(d, t, p))
+            if t > 1:
+                for d in range(2):
+                    when(has(d, t - 1), lambda d=d, p=p, t=t: q_cross(d, t - 1, p))
+        if t == last:
+            for p in range(O_PARTS):
+                for d in range(2):
+                    when(can_go[d], lambda d=d, p=p: o_on(d, 0, p).start())
+    for p in range(O_PARTS):
+        o_cross(0, 0, p)
     for d in range(2):
-        when(can_go[d], lambda d=d: o_on(d, 0).start())
-    o_y(0, 0).start()
-    if last > 0:
-        for d in range(2):
-            when(has(d, last), lambda d=d: cross(d, last))
+        each(has(d, last), Q_PARTS, lambda p, d=d: q_cross(d, last, p))
     for t in range(1, last + 1):
-        for d in range(2):
-            when(has(d, t), lambda d=d, t=t: o_arrive(d, t))
-        if t == 1:
-            o_cross(0, 0)
-        else:
+        for p in range(O_PARTS):
             for d in range(2):
-                when(has(d, t - 1), lambda d=d, t=t: o_cross(d, t - 1))
+                when(has(d, t), lambda d=d, p=p, t=t: o_arrive(d, t, p))
+            if t > 1:
+                for d in range(2):
+                    when(has(d, t - 1), lambda d=d, p=p, t=t: o_cross(d, t - 1, p))
     for d in range(2):
-        when(has(d, last), lambda d=d: o_cross(d, last))
+        each(has(d, last), O_PARTS, lambda p, d=d: o_cross(d, last, p))
 
     for copy in mine:
         copy.wait()
-    v_copy.wait_send()
-    remote(video, v_peer, vs, vr, blk, yp).wait_recv()
-    o_y(0, 0).wait_send()
-    o_d(0, 0).wait_send()
-    o_din(0, 0).wait_recv()
+    for p in range(V_PARTS):
+        v_out(p).wait_send()
+        v_in(p).wait_recv()
+    for p in range(O_PARTS):
+        o_y(0, 0, p).wait_send()
+        o_d(0, 0, p).wait_send()
+        o_din(0, 0, p).wait_recv()
+
+    def q_end(d, t, p):
+        q_x(d, t, p).wait_send()
+        q_c(d, t, p).wait_send()
+        q_d(d, t, p).wait_send()
+        q_cin(d, t, p).wait_recv()
+        q_din(d, t, p).wait_recv()
+
+    def o_end(d, t, p):
+        o_y(d, t, p).wait_send()
+        o_c(d, t, p).wait_send()
+        o_d(d, t, p).wait_send()
+        o_cin(d, t, p).wait_recv()
+        o_din(d, t, p).wait_recv()
+
     for d in range(2):
-        when(
-            can_go[d],
-            lambda d=d: remote(
-                q_own, q_at(a, c), zs.at[d, 0], zr.at[d, 0], blk, onward[d]
-            ).wait_send(),
-        )
-        when(can_go[d], lambda d=d: o_on(d, 0).wait_send())
-
-        def finish(d, t):
-            if t < last:
-                when(can_go[d], lambda: q_on(d, t).wait_send())
-                when(can_go[d], lambda: o_on(d, t).wait_send())
-            q_x(d, t).wait_send()
-            q_c(d, t).wait_send()
-            q_d(d, t).wait_send()
-            q_cin(d, t, c + 1 - 2 * core, cs, cr).wait_recv()
-            q_cin(d, t, x_c + 1 - 2 * core, ds, dr).wait_recv()
-            o_y(d, t).wait_send()
-            o_c(d, t).wait_send()
-            o_d(d, t).wait_send()
-            o_cin(d, t).wait_recv()
-            o_din(d, t).wait_recv()
-
+        for t in range(last):
+            on = can_go[d] if t == 0 else jnp.logical_and(has(d, t), can_go[d])
+            each(on, Q_PARTS, lambda p, d=d, t=t: q_on(d, t, p).wait_send())
+            each(on, O_PARTS, lambda p, d=d, t=t: o_on(d, t, p).wait_send())
         for t in range(1, last + 1):
-            when(has(d, t), lambda d=d, t=t: finish(d, t))
+            each(has(d, t), Q_PARTS, lambda p, d=d, t=t: q_end(d, t, p))
+            each(has(d, t), O_PARTS, lambda p, d=d, t=t: o_end(d, t, p))
 
 
 def gather_weights(video, wq, wo, groups):
     rows = video.shape[0]
-    pair = pltpu.SemaphoreType.DMA((2, groups))
+    q_sems = pltpu.SemaphoreType.DMA((2, groups * Q_PARTS))
+    o_sems = pltpu.SemaphoreType.DMA((2, groups * O_PARTS))
     return pl.pallas_call(
         functools.partial(gather_kernel, groups),
         out_shape=(
@@ -282,10 +298,11 @@
         out_specs=(ANY,) * 3,
         scratch_shapes=[
             pltpu.SemaphoreType.DMA((3,)),
-            pltpu.SemaphoreType.DMA,
-            pltpu.SemaphoreType.DMA,
+            pltpu.SemaphoreType.DMA((V_PARTS,)),
+            pltpu.SemaphoreType.DMA((V_PARTS,)),
         ]
-        + [pair] * 16,
+        + [q_sems] * 8
+        + [o_sems] * 8,
         compiler_params=pltpu.CompilerParams(collective_id=0, has_side_effects=True),
     )(video, wq, wo)
 

time: 214 us -> 217 us (1.014)
  Pallas kernels: 178 us -> 181 us
    pallas_call x1, Pallas kernels: 136 us -> 138 us  [gather_weights(): pl.pallas_call(functools.partial(gather_kernel, groups), out_shape=(jax.S...]
where the time goes in v2:
time: 217 us; the launch traced here: 216 us
  Pallas kernels  181 us (83%)
  blocking collectives  17.3 us (8%)
  matrix products  12.4 us (6%)
  local copies, waits for them, and re-layouts  2.92 us (1%)
  other arithmetic  2.77 us (1%)
    pallas_call x1, Pallas kernels, gather_weights(): pl.pallas_call(functools.partial(gather_kernel, groups), out_shape=(jax.S...  138 us
    pallas_call x1, Pallas kernels, exchange_heads(): pl.pallas_call(functools.partial(exchange_kernel, groups, slabs), out_sha...  30 us
    all_to_all x1, blocking collectives, local(): lax.all_to_all(attended.reshape(ranks, video.shape[0], head_size), 'uly',...  17.3 us
    pallas_call x1, Pallas kernels, attend(): pl.pallas_call(functools.partial(attend_kernel, head_size), out_shape=jax...  12.7 us
    dot_general x1, matrix products, local(): jnp.einsum('td,adn->atn', rows2, w_all, preferred_element_type=jnp.float32)  7.13 us
    dot_general x1, matrix products, local(): jnp.dot(by_token, wo_all.reshape(ranks * head_size, w_out.shape[1]), pref...  5.28 us

profile of v2, /device:TPU:1, one launch (start us, length us, event | category | flops | bytes accessed | tf_op | source)
XLA Modules:
  0.0 216.3 jit_solution(15696714659187067462)
XLA Ops:
  0.0 138.0 %shard_map.73 = (bf16[384,3072]{1,0:T(8,128)(2,1)}, bf16[4,3072,384]{2,1,0:T(8,128)(2,1)}, bf16[8,128,3072]{2,1,0:T(8,128)(2,1)}) custom-call(bf16[192,3072]{1,0:T(8,128)(2,1)} %video.1, bf16[3072,384]{1,0:T(8,128)(2,1)} %wq.1, bf16[128,3072]{1,0:T(8,128)(2,1)} %wo.1), custom_call_target="tpu_custom_call" | custom-call | tf_op jit(solution)/shard_map/pallas_call | solution.py:290
  138.0 7.1 %fusion.3 = f32[4,384,384]{2,1,0:T(8,128)S(1)} fusion(bf16[4,3072,384]{2,1,0:T(8,128)(2,1)} %get-tuple-element.10, bf16[384,3072]{1,0:T(8,128)(2,1)} %get-tuple-element.11), kind=kOutput, calls=%fused_computation.4 | convolution fusion | flops 3623878656 | bytes 14155776 | tf_op jit(solution)/shard_map/td,adn->atn/dot_general | solution.py:486
  145.2 0.0 copy-start.3
  145.2 0.0 copy-start.4
  145.2 0.0 copy-start.5
  145.2 0.5 multiply_reduce_fusion
  145.7 0.1 slice.26
  145.8 0.1 copy-done.3
  145.9 0.1 slice.17
  146.0 0.1 pad_add_fusion.ids
  146.1 0.0 copy-done.4
  146.1 0.0 copy-done.5
  146.1 0.0 copy-start.2
  146.1 1.2 multiply_convert_fusion
  147.3 1.0 pad_maximum_fusion.kv
  148.3 30.0 %shard_map.74 = (bf16[4,384,128]{2,1,0:T(8,128)(2,1)}, bf16[3,4,384,256]{3,2,1,0:T(8,128)(2,1)}) custom-call(bf16[4,384,128]{2,1,0:T(8,128)(2,1)} %get-tuple-element.18.q, bf16[4,384,256]{2,1,0:T(8,128)(2,1)} %pad_maximum_fusion.kv), custom_call_target="tpu_custom_call" | custom-call | tf_op jit(solution)/shard_map/pallas_call | solution.py:404
  178.3 0.0 copy-done.2
  178.3 0.0 copy-start
  178.3 1.7 copy-done
  180.0 0.0 copy-start.1
  180.0 1.0 copy-done.1
  181.0 12.7 %shard_map.75 = bf16[1536,128]{1,0:T(8,128)(2,1)S(1)} custom-call(s32[24,28]{1,0:T(8,128)S(1)} %pad_add_fusion.ids, s32[24]{0:T(128)S(1)} %copy-done.2, bf16[1536,128]{1,0:T(8,128)(2,1)S(1)} %bitcast.21, bf16[4608,256]{1,0:T(8,128)(2,1)S(1)} %bitcast.19), custom_call_target="tpu_custom_call" | custom-call | tf_op jit(solution)/shard_map/pallas_call | solution.py:454
  193.7 17.3 %all_to_all.5 = bf16[8,192,128]{2,1,0:T(8,128)(2,1)S(1)} all-to-all(bf16[8,192,128]{2,1,0:T(8,128)(2,1)S(1)} %bitcast.20), channel_id=1, replica_groups=mesh['blk'=4,'uly'=8] {'uly'}, dimensions={0} | all-to-all | bytes 786432 | tf_op jit(solution)/shard_map/all_to_all | solution.py:503
  211.0 5.3 %fusion = bf16[192,3072]{1,0:T(8,128)(2,1)} fusion(bf16[8,128,3072]{2,1,0:T(8,128)(2,1)} %get-tuple-element.14, bf16[8,192,128]{2,1,0:T(8,128)(2,1)S(1)} %all_to_all.5), kind=kOutput, calls=%fused_computation.1 | convolution fusion | flops 1208549376 | bytes 7864320 | tf_op jit(solution)/shard_map/dot_general | solution.py:507
  (2 shorter events, 0.0 us)
Async XLA Ops:
  145.2 0.7 copy-start.3
  145.2 0.9 copy-start.4
  145.2 0.9 copy-start.5
  146.1 32.2 %copy-start.2 = (s32[24]{0:T(128)S(1)}, s32[24]{0:T(128)}, u32[]{:S(2)}) copy-start(s32[24]{0:T(128)} %counts.1) | copy-start | bytes 292
  178.3 1.7 copy-start
  180.0 1.0 copy-start.1

commit v3 on v2

--- a/solution.py
+++ b/solution.py
@@ -26,6 +26,19 @@
         device_id=(blk, uly),
         device_id_type=MESH,
     )
+
+
+def through_vmem(sources, targets, rooms, sems):
+    count = len(sources)
+    ins = [pltpu.make_async_copy(sources[i], rooms[i], sems.at[i]) for i in range(count)]
+    for copy in ins:
+        copy.start()
+    outs = []
+    for i in range(count):
+        ins[i].wait()
+        outs.append(pltpu.make_async_copy(rooms[i], targets[i], sems.at[count + i]))
+        outs[i].start()
+    return outs
 
 
 def when(cond, fn):
@@ -59,6 +72,9 @@
     ocr,
     ods,
     odr,
+    wq_v,
+    video_v,
+    wo_v,
 ):
     blk, uly = lax.axis_index("blk"), lax.axis_index("uly")
     a, y = uly // 2, uly % 2
@@ -214,15 +230,13 @@
         v_out(p).start()
     for p in range(O_PARTS):
         o_y(0, 0, p).start()
-    mine = [
-        pltpu.make_async_copy(wq, wq_all.at[a], local_sem.at[0]),
-        pltpu.make_async_copy(
-            video, vid2.at[pl.ds(pl.multiple_of(y * rows, 16), rows)], local_sem.at[1]
-        ),
-        pltpu.make_async_copy(wo, wo_all.at[uly], local_sem.at[2]),
-    ]
-    for copy in mine:
-        copy.start()
+    y_rows = pl.ds(pl.multiple_of(y * rows, 16), rows)
+    mine = through_vmem(
+        (wq, video, wo),
+        (wq_all.at[a], vid2.at[y_rows], wo_all.at[uly]),
+        (wq_v, video_v, wo_v),
+        local_sem,
+    )
 
     for t in range(1, last + 1):
         for p in range(Q_PARTS):
@@ -297,17 +311,20 @@
         in_specs=[ANY] * 3,
         out_specs=(ANY,) * 3,
         scratch_shapes=[
-            pltpu.SemaphoreType.DMA((3,)),
+            pltpu.SemaphoreType.DMA((6,)),
             pltpu.SemaphoreType.DMA((V_PARTS,)),
             pltpu.SemaphoreType.DMA((V_PARTS,)),
         ]
         + [q_sems] * 8
-        + [o_sems] * 8,
-        compiler_params=pltpu.CompilerParams(collective_id=0, has_side_effects=True),
+        + [o_sems] * 8
+        + [pltpu.VMEM(block.shape, block.dtype) for block in (wq, video, wo)],
+        compiler_params=pltpu.CompilerParams(
+            collective_id=0, has_side_effects=True, vmem_limit_bytes=48 << 20
+        ),
     )(video, wq, wo)
 
 
-def exchange_kernel(groups, slabs, q, kv, q_all, kv_all, local_sem, qs, qr, ks, kr, ps, pr, ns, nr):
+def exchange_kernel(groups, slabs, q, kv, q_all, kv_all, local_sem, qs, qr, ks, kr, ps, pr, ns, nr, q_v, kv_v):
     blk, uly = lax.axis_index("blk"), lax.axis_index("uly")
     a, y = uly // 2, uly % 2
     has_prev, has_next = blk > 0, blk < slabs - 1
@@ -367,14 +384,11 @@
         kv_out(k).start()
     when(has_prev, lambda: to_prev(0).start())
     when(has_next, lambda: to_next(0).start())
-    mine = [
-        pltpu.make_async_copy(q.at[a], q_all.at[a], local_sem.at[0]),
-        pltpu.make_async_copy(kv.at[a], kv_all.at[1, a], local_sem.at[1]),
-    ]
-    for copy in mine:
-        copy.start()
     for k in range(1, groups):
         q_out(k).start()
+    mine = through_vmem(
+        (q.at[a], kv.at[a]), (q_all.at[a], kv_all.at[1, a]), (q_v, kv_v), local_sem
+    )
     for k in range(1, groups):
         kv_in(k).wait_recv()
         when(has_prev, lambda k=k: to_prev(k).start())
@@ -409,8 +423,12 @@
         ),
         in_specs=[ANY] * 2,
         out_specs=(ANY,) * 2,
-        scratch_shapes=[pltpu.SemaphoreType.DMA((2,))] + [sems] * 8,
-        compiler_params=pltpu.CompilerParams(collective_id=1, has_side_effects=True),
+        scratch_shapes=[pltpu.SemaphoreType.DMA((4,))]
+        + [sems] * 8
+        + [pltpu.VMEM(block.shape[1:], block.dtype) for block in (q, kv)],
+        compiler_params=pltpu.CompilerParams(
+            collective_id=1, has_side_effects=True, vmem_limit_bytes=48 << 20
+        ),
     )(q, kv)
 
 

time: 217 us -> 155 us (0.71)
  Pallas kernels: 181 us -> 123 us
  matrix products: 12.4 us -> 8.84 us
    pallas_call x1, Pallas kernels: 138 us -> 83.5 us  [gather_weights(): pl.pallas_call(functools.partial(gather_kernel, groups), out_shape=(jax.S...]
    pallas_call x1, Pallas kernels: 30 us -> 27 us  [exchange_heads(): pl.pallas_call(functools.partial(exchange_kernel, groups, slabs), out_sha...]
    dot_general x1, matrix products: 5.28 us -> 2.49 us  [local(): jnp.dot(by_token, wo_all.reshape(ranks * head_size, w_out.shape[1]), pref...]
where the time goes in v3:
time: 155 us; the launch traced here: 154 us
  Pallas kernels  123 us (79%)
  blocking collectives  18 us (12%)
  matrix products  8.84 us (6%)
  local copies, waits for them, and re-layouts  2.67 us (2%)
    pallas_call x1, Pallas kernels, gather_weights(): pl.pallas_call(functools.partial(gather_kernel, groups), out_shape=(jax.S...  83.5 us
    pallas_call x1, Pallas kernels, exchange_heads(): pl.pallas_call(functools.partial(exchange_kernel, groups, slabs), out_sha...  27 us
    all_to_all x1, blocking collectives, local(): lax.all_to_all(attended.reshape(ranks, video.shape[0], head_size), 'uly',...  18 us
    pallas_call x1, Pallas kernels, attend(): pl.pallas_call(functools.partial(attend_kernel, head_size), out_shape=jax...  12.9 us
    dot_general x1, matrix products, local(): jnp.einsum('td,adn->atn', rows2, w_all, preferred_element_type=jnp.float32)  6.35 us

profile of v3, /device:TPU:1, one launch (start us, length us, event | category | flops | bytes accessed | tf_op | source)
XLA Modules:
  0.0 154.3 jit_solution(11207220625251143715)
XLA Ops:
  0.0 1.3 copy-done
  1.3 1.1 copy-done.1
  2.4 83.5 %shard_map.73 = (bf16[384,3072]{1,0:T(8,128)(2,1)S(1)}, bf16[4,3072,384]{2,1,0:T(8,128)(2,1)}, bf16[8,128,3072]{2,1,0:T(8,128)(2,1)}) custom-call(bf16[192,3072]{1,0:T(8,128)(2,1)S(1)} %copy-done, bf16[3072,384]{1,0:T(8,128)(2,1)} %wq.1, bf16[128,3072]{1,0:T(8,128)(2,1)S(1)} %copy-done.1), custom_call_target="tpu_custom_call" | custom-call | tf_op jit(solution)/shard_map/pallas_call | solution.py:304
  86.0 6.3 %fusion.3 = f32[4,384,384]{2,1,0:T(8,128)S(1)} fusion(bf16[4,3072,384]{2,1,0:T(8,128)(2,1)} %get-tuple-element.10, bf16[384,3072]{1,0:T(8,128)(2,1)S(1)} %get-tuple-element.11), kind=kOutput, calls=%fused_computation.4 | convolution fusion | flops 3623878656 | bytes 14155776 | tf_op jit(solution)/shard_map/td,adn->atn/dot_general | solution.py:504
  92.3 0.0 copy-start.3
  92.3 0.0 copy-start.4
  92.3 0.0 copy-start.5
  92.3 0.5 multiply_reduce_fusion
  92.8 0.1 slice.26
  92.9 0.1 copy-done.3
  93.0 0.1 slice.17
  93.1 0.1 pad_add_fusion.ids
  93.2 0.0 copy-done.4
  93.2 0.0 copy-done.5
  93.2 0.0 copy-start.2
  93.2 0.5 multiply_convert_fusion
  93.7 0.0 copy-start.6
  93.7 0.1 pad_maximum_fusion.kv
  93.8 27.0 %shard_map.74 = (bf16[4,384,128]{2,1,0:T(8,128)(2,1)S(1)}, bf16[3,4,384,256]{3,2,1,0:T(8,128)(2,1)S(1)}) custom-call(bf16[4,384,128]{2,1,0:T(8,128)(2,1)S(1)} %get-tuple-element.18.q, bf16[4,384,256]{2,1,0:T(8,128)(2,1)S(1)} %pad_maximum_fusion.kv), custom_call_target="tpu_custom_call" | custom-call | tf_op jit(solution)/shard_map/pallas_call | solution.py:418
  120.9 0.0 copy-done.2
  120.9 12.9 %shard_map.75 = bf16[1536,128]{1,0:T(8,128)(2,1)S(1)} custom-call(s32[24,28]{1,0:T(8,128)S(1)} %pad_add_fusion.ids, s32[24]{0:T(128)S(1)} %copy-done.2, bf16[1536,128]{1,0:T(8,128)(2,1)S(1)} %bitcast.21, bf16[4608,256]{1,0:T(8,128)(2,1)S(1)} %bitcast.19), custom_call_target="tpu_custom_call" | custom-call | tf_op jit(solution)/shard_map/pallas_call | solution.py:472
  133.8 18.0 %all_to_all.5 = bf16[8,192,128]{2,1,0:T(8,128)(2,1)S(1)} all-to-all(bf16[8,192,128]{2,1,0:T(8,128)(2,1)S(1)} %bitcast.20), channel_id=1, replica_groups=mesh['blk'=4,'uly'=8] {'uly'}, dimensions={0} | all-to-all | bytes 786432 | tf_op jit(solution)/shard_map/all_to_all | solution.py:521
  151.8 0.0 copy-done.6
  151.8 2.5 %fusion = bf16[192,3072]{1,0:T(8,128)(2,1)} fusion(bf16[8,128,3072]{2,1,0:T(8,128)(2,1)S(1)} %copy-done.6, bf16[8,192,128]{2,1,0:T(8,128)(2,1)S(1)} %all_to_all.5), kind=kOutput, calls=%fused_computation.1 | convolution fusion | flops 1208549376 | bytes 7864320 | tf_op jit(solution)/shard_map/dot_general | solution.py:525
  (4 shorter events, 0.0 us)
Async XLA Ops:
  0.0 1.3 copy-start
  1.3 1.1 copy-start.1
  92.3 0.7 copy-start.3
  92.3 0.9 copy-start.4
  92.3 0.9 copy-start.5
  93.2 27.7 %copy-start.2 = (s32[24]{0:T(128)S(1)}, s32[24]{0:T(128)}, u32[]{:S(2)}) copy-start(s32[24]{0:T(128)} %counts.1) | copy-start | bytes 292
  93.7 58.1 %copy-start.6 = (bf16[8,128,3072]{2,1,0:T(8,128)(2,1)S(1)}, bf16[8,128,3072]{2,1,0:T(8,128)(2,1)}, u32[]{:S(2)}) copy-start(bf16[8,128,3072]{2,1,0:T(8,128)(2,1)} %get-tuple-element.14) | copy-start | bytes 18874372

commit v4 on v3

--- a/solution.py
+++ b/solution.py
@@ -11,7 +11,7 @@
 BLOCK = 64
 CHUNK = 4
 Q_PARTS = 4
-O_PARTS = 2
+O_PARTS = 4
 V_PARTS = 2
 MESH = pl.DeviceIdType.MESH
 ANY = pl.BlockSpec(memory_space=pl.ANY)
@@ -245,7 +245,7 @@
             if t > 1:
                 for d in range(2):
                     when(has(d, t - 1), lambda d=d, p=p, t=t: q_cross(d, t - 1, p))
-        if t == last:
+        if t == 1:
             for p in range(O_PARTS):
                 for d in range(2):
                     when(can_go[d], lambda d=d, p=p: o_on(d, 0, p).start())

time: 155 us -> 161 us (1.039)
  Pallas kernels: 123 us -> 130 us
    pallas_call x1, Pallas kernels: 83.5 us -> 90.1 us  [gather_weights(): pl.pallas_call(functools.partial(gather_kernel, groups), out_shape=(jax.S...]
where the time goes in v4:
time: 161 us
  Pallas kernels  130 us (81%)
  blocking collectives  18.4 us (11%)
  matrix products  8.85 us (5%)
  local copies, waits for them, and re-layouts  2.67 us (2%)
    pallas_call x1, Pallas kernels, gather_weights(): pl.pallas_call(functools.partial(gather_kernel, groups), out_shape=(jax.S...  90.1 us
    pallas_call x1, Pallas kernels, exchange_heads(): pl.pallas_call(functools.partial(exchange_kernel, groups, slabs), out_sha...  26.7 us
    all_to_all x1, blocking collectives, local(): lax.all_to_all(attended.reshape(ranks, video.shape[0], head_size), 'uly',...  18.4 us
    pallas_call x1, Pallas kernels, attend(): pl.pallas_call(functools.partial(attend_kernel, head_size), out_shape=jax...  12.9 us
    dot_general x1, matrix products, local(): jnp.einsum('td,adn->atn', rows2, w_all, preferred_element_type=jnp.float32)  6.35 us

profile of v4, /device:TPU:1, one launch (start us, length us, event | category | flops | bytes accessed | tf_op | source)
XLA Modules:
  0.0 160.9 jit_solution(7440776007239705717)
XLA Ops:
  0.0 1.3 copy-done
  1.3 1.1 copy-done.1
  2.4 90.1 %shard_map.73 = (bf16[384,3072]{1,0:T(8,128)(2,1)S(1)}, bf16[4,3072,384]{2,1,0:T(8,128)(2,1)}, bf16[8,128,3072]{2,1,0:T(8,128)(2,1)}) custom-call(bf16[192,3072]{1,0:T(8,128)(2,1)S(1)} %copy-done, bf16[3072,384]{1,0:T(8,128)(2,1)} %wq.1, bf16[128,3072]{1,0:T(8,128)(2,1)S(1)} %copy-done.1), custom_call_target="tpu_custom_call" | custom-call | tf_op jit(solution)/shard_map/pallas_call | solution.py:304
  92.5 6.3 %fusion.3 = f32[4,384,384]{2,1,0:T(8,128)S(1)} fusion(bf16[4,3072,384]{2,1,0:T(8,128)(2,1)} %get-tuple-element.10, bf16[384,3072]{1,0:T(8,128)(2,1)S(1)} %get-tuple-element.11), kind=kOutput, calls=%fused_computation.4 | convolution fusion | flops 3623878656 | bytes 14155776 | tf_op jit(solution)/shard_map/td,adn->atn/dot_general | solution.py:504
  98.9 0.0 copy-start.3
  98.9 0.0 copy-start.4
  98.9 0.0 copy-start.5
  98.9 0.5 multiply_reduce_fusion
  99.4 0.1 slice.26
  99.5 0.1 copy-done.3
  99.6 0.1 slice.17
  99.7 0.1 pad_add_fusion.ids
  99.8 0.0 copy-done.4
  99.8 0.0 copy-done.5
  99.8 0.0 copy-start.2
  99.8 0.5 multiply_convert_fusion
  100.3 0.0 copy-start.6
  100.3 0.1 pad_maximum_fusion.kv
  100.4 26.7 %shard_map.74 = (bf16[4,384,128]{2,1,0:T(8,128)(2,1)S(1)}, bf16[3,4,384,256]{3,2,1,0:T(8,128)(2,1)S(1)}) custom-call(bf16[4,384,128]{2,1,0:T(8,128)(2,1)S(1)} %get-tuple-element.18.q, bf16[4,384,256]{2,1,0:T(8,128)(2,1)S(1)} %pad_maximum_fusion.kv), custom_call_target="tpu_custom_call" | custom-call | tf_op jit(solution)/shard_map/pallas_call | solution.py:418
  127.1 0.0 copy-done.2
  127.1 12.9 %shard_map.75 = bf16[1536,128]{1,0:T(8,128)(2,1)S(1)} custom-call(s32[24,28]{1,0:T(8,128)S(1)} %pad_add_fusion.ids, s32[24]{0:T(128)S(1)} %copy-done.2, bf16[1536,128]{1,0:T(8,128)(2,1)S(1)} %bitcast.21, bf16[4608,256]{1,0:T(8,128)(2,1)S(1)} %bitcast.19), custom_call_target="tpu_custom_call" | custom-call | tf_op jit(solution)/shard_map/pallas_call | solution.py:472
  140.0 18.4 %all_to_all.5 = bf16[8,192,128]{2,1,0:T(8,128)(2,1)S(1)} all-to-all(bf16[8,192,128]{2,1,0:T(8,128)(2,1)S(1)} %bitcast.20), channel_id=1, replica_groups=mesh['blk'=4,'uly'=8] {'uly'}, dimensions={0} | all-to-all | bytes 786432 | tf_op jit(solution)/shard_map/all_to_all | solution.py:521
  158.4 0.0 copy-done.6
  158.4 2.5 %fusion = bf16[192,3072]{1,0:T(8,128)(2,1)} fusion(bf16[8,128,3072]{2,1,0:T(8,128)(2,1)S(1)} %copy-done.6, bf16[8,192,128]{2,1,0:T(8,128)(2,1)S(1)} %all_to_all.5), kind=kOutput, calls=%fused_computation.1 | convolution fusion | flops 1208549376 | bytes 7864320 | tf_op jit(solution)/shard_map/dot_general | solution.py:525
  (4 shorter events, 0.0 us)
Async XLA Ops:
  0.0 1.3 copy-start
  1.3 1.1 copy-start.1
  98.9 0.7 copy-start.3
  98.9 0.9 copy-start.4
  98.9 0.9 copy-start.5
  99.8 27.3 %copy-start.2 = (s32[24]{0:T(128)S(1)}, s32[24]{0:T(128)}, u32[]{:S(2)}) copy-start(s32[24]{0:T(128)} %counts.1) | copy-start | bytes 292
  100.3 58.1 %copy-start.6 = (bf16[8,128,3072]{2,1,0:T(8,128)(2,1)S(1)}, bf16[8,128,3072]{2,1,0:T(8,128)(2,1)}, u32[]{:S(2)}) copy-start(bf16[8,128,3072]{2,1,0:T(8,128)(2,1)} %get-tuple-element.14) | copy-start | bytes 18874372
